TPU v7x, 1024 devices: a whole 4x4x32 slice. The times are simulated.
1024 devices in a mesh: dp: 16 (over x, y), expert: 64 (over z, core).
Axes of the slice: x: 4, y: 4, z: 32, core: 2. Of those that a mesh axis runs over, the one named last changes fastest.
Arguments:
- tokens: bfloat16 [2048, 64, 1024], P(('dp', 'expert')), may hold values from -8 to 8
- expert_ids: int32 [2048, 64, 1], P(('dp', 'expert')), may hold values from 0 to 31; in each aligned block of 128 rows (0 to 127, 128 to 255, ..., all dimensions but the last counted through in order) at most 6 rows name the same one
- caption_len: int32 [2048], P(('dp', 'expert')), may hold values from 1 to 16, as said below
- router: bfloat16 [1024, 32], replicated, may hold values from -0.1875 to 0.1875
- expert_in: bfloat16 [64, 1024, 2048], P('expert'), may hold values from -0.1875 to 0.1875
- expert_out: bfloat16 [64, 2048, 1024], P('expert'), may hold values from -0.09375 to 0.09375
Outputs:
- layer_out: bfloat16 [2048, 64, 1024], P(('dp', 'expert'))
- pair_loss: float32 [2048], P(('dp', 'expert'))
Inputs may be any that keep to these rules, and one draw needn't show every extreme that they name: `expert_ids`: in the 128 tokens of one device no expert is named more than 6 times, a bound that some block reaches. `caption_len`: the first pair of every device has a caption of full length.
All inputs are finite; a program needn't handle non-finite values.
Results may differ from a plain program's by a relative error of at most 0.008.
Values may be sent and summed in bfloat16 or wider, within the bound.
A program may use at most 64 MiB of HBM per device.

v0:
```python
import jax
import jax.numpy as jnp
from jax import lax
from jax.sharding import PartitionSpec as P

IMG_TOK = 48
TXT_TOK = 16


logit_scale = 20.0
norm_eps = 1e-06


def unit_rows(vectors):
    squared_total = jnp.sum(vectors * vectors, axis=-1, keepdims=True) + norm_eps
    return (vectors * lax.rsqrt(squared_total)).astype(jnp.bfloat16)


def per_device(tokens, expert_ids, caption_len, router, expert_in, expert_out):
    pair_count, seq_len, model_width = tokens.shape
    token_rows = tokens.reshape(pair_count * seq_len, model_width)
    row_count = token_rows.shape[0]
    chosen_ids = expert_ids.reshape(row_count)
    expert_count = router.shape[1]
    capacity = 2 * ((3 * row_count + 4 * expert_count - 1) // (4 * expert_count))
    onehot = chosen_ids[:, None] == jnp.arange(expert_count, dtype=jnp.int32)[None, :]
    running = jnp.cumsum(onehot.astype(jnp.int32), axis=0) - 1
    position = jnp.sum(jnp.where(onehot, running, 0), axis=1)
    slot_index = chosen_ids * capacity + position
    slot_mask = (
        slot_index[:, None] == jnp.arange(expert_count * capacity, dtype=jnp.int32)[None, :]
    ).astype(jnp.bfloat16)
    outgoing = lax.dot_general(
        slot_mask, token_rows, (((0,), (0,)), ((), ())), preferred_element_type=jnp.float32
    ).astype(jnp.bfloat16)
    logits = jnp.dot(token_rows, router, preferred_element_type=jnp.float32)
    gate_value = jax.nn.sigmoid(jnp.sum(jnp.where(onehot, logits, 0.0), axis=1))
    first_layer = expert_in[0]
    second_layer = expert_out[0]

    def partial_value(incoming):
        hidden = jax.nn.gelu(
            jnp.dot(incoming, first_layer, preferred_element_type=jnp.float32)
        ).astype(jnp.bfloat16)
        return jnp.dot(hidden, second_layer, preferred_element_type=jnp.float32).astype(
            jnp.bfloat16
        )

    owners = 2 * expert_count
    doubled = jnp.broadcast_to(
        outgoing.reshape(expert_count, 1, capacity, model_width),
        (expert_count, 2, capacity, model_width),
    ).reshape(owners, capacity, model_width)
    arrived = lax.all_to_all(doubled, "expert", split_axis=0, concat_axis=0, tiled=True)
    partial_value = partial_value(arrived.reshape(owners * capacity, model_width)).reshape(
        owners, capacity, model_width
    )
    returned = (
        lax.all_to_all(partial_value, "expert", split_axis=0, concat_axis=0, tiled=True)
        .reshape(expert_count, 2, capacity, model_width)
        .astype(jnp.float32)
    )
    slot_values = (
        (returned[:, 0] + returned[:, 1])
        .astype(jnp.bfloat16)
        .reshape(expert_count * capacity, model_width)
    )
    token_values = jnp.dot(slot_mask, slot_values, preferred_element_type=jnp.float32)
    layer_out = (token_rows.astype(jnp.float32) + gate_value[:, None] * token_values).astype(
        jnp.bfloat16
    )
    pooled_source = layer_out.reshape(pair_count, seq_len, model_width).astype(jnp.float32)
    image_vec = jnp.mean(pooled_source[:, :IMG_TOK, :], axis=1)
    text_mask = (jnp.arange(TXT_TOK, dtype=jnp.int32)[None, :] < caption_len[:, None]).astype(
        jnp.float32
    )
    text_vec = jnp.sum(pooled_source[:, IMG_TOK:, :] * text_mask[:, :, None], axis=1) / caption_len[
        :, None
    ].astype(jnp.float32)
    image_unit = unit_rows(image_vec)
    text_unit = unit_rows(text_vec)
    scores = logit_scale * lax.dot_general(
        image_unit,
        lax.all_gather(text_unit, ("dp", "expert"), axis=0, tiled=True),
        (((1,), (1,)), ((), ())),
        preferred_element_type=jnp.float32,
    )
    weights = jnp.exp(scores)
    column_sums = jnp.sum(weights, axis=0)
    row_sums, column_sums = (jnp.sum(weights, axis=1), column_sums)
    every_column = lax.psum(column_sums, ("dp", "expert"))
    own_columns = lax.dynamic_slice_in_dim(
        every_column, lax.axis_index(("dp", "expert")) * pair_count, pair_count
    )
    matched = logit_scale * jnp.sum(
        image_unit.astype(jnp.float32) * text_unit.astype(jnp.float32), axis=1
    )
    pair_loss = 0.5 * (jnp.log(row_sums) - matched) + 0.5 * (jnp.log(own_columns) - matched)
    return (layer_out.reshape(pair_count, seq_len, model_width), pair_loss)


def solution(mesh):
    return jax.shard_map(
        per_device,
        mesh=mesh,
        in_specs=(
            P(("dp", "expert"), None, None),
            P(("dp", "expert"), None, None),
            P(("dp", "expert")),
            P(),
            P("expert", None, None),
            P("expert", None, None),
        ),
        out_specs=(P(("dp", "expert"), None, None), P(("dp", "expert"))),
        check_vma=False,
    )
```

profile of v0, /device:TPU:6, one launch (start us, length us, event | category | flops | bytes accessed | tf_op | source)
XLA Modules:
  0.0 805.5 jit_solution(4394017939868641449)
XLA Ops:
  7.2 0.5 broadcast.69
  7.7 1.3 reduce.3
  9.0 0.1 eq.28
  9.1 0.1 copy.14
  9.2 0.2 reduce_window_sum.11
  9.4 0.1 copy.15
  9.5 1.3 convolution_convert_fusion
  10.8 0.1 broadcast_in_dim.14
  11.0 0.1 broadcast_in_dim.15
  11.1 139.8 %all_to_all.10 = bf16[64,6,1024]{2,1,0:T(8,128)(2,1)S(1)} all-to-all(bf16[64,6,1024]{2,1,0:T(8,128)(2,1)S(1)} %bitcast.40), channel_id=1, replica_groups=mesh['dp'=16,'expert'=64] {'expert'}, dimensions={0} | all-to-all | bytes 1572864 | tf_op jit(solution)/shard_map/all_to_all | solution.py:54
  150.9 0.3 reshape.84
  151.2 7.1 fusion.15
  158.3 1.2 reshape.85
  159.5 4.7 all-to-all-start.1
  164.2 0.0 all-gather.3.cloned.1.call-start
  164.3 0.2 fusion.20
  164.5 0.1 compare_convert_fusion
  164.6 110.3 %all-to-all-done.1 = bf16[64,6,1024]{2,1,0:T(8,128)(2,1)S(1)} async-done(((bf16[64,6,1024]{2,1,0:T(8,128)(2,1)}), bf16[64,6,1024]{2,1,0:T(8,128)(2,1)S(1)}, u32[]{:S(2)}, u32[]{:S(2)}) %all-to-all-start.1) | async-done | bytes 786464 | tf_op jit(solution)/shard_map/all_to_all | solution.py:59
  274.9 0.2 convert.1
  275.1 0.1 fusion.22
  275.3 0.1 convert_element_type.66
  275.4 0.3 fusion.19
  275.8 0.1 fusion.25
  275.9 0.1 multiply_reduce_fusion.2
  276.0 0.2 multiply_reduce_fusion.1
  276.2 0.8 multiply_reduce_fusion
  277.0 0.0 all-gather.3.cloned.1.call-update
  277.1 357.0 %all-gather.3.cloned.1.call-done = bf16[1024,2,1024]{2,1,0:T(2,128)(2,1)} async-done(((bf16[1,2,1024]{2,1,0:T(2,128)(2,1)}), bf16[1024,2,1024]{2,1,0:T(2,128)(2,1)}) %all-gather.3.cloned.1.call-update) | async-done | bytes 4194320 | tf_op jit(solution)/shard_map/all_gather | solution.py:84
  634.1 7.2 reshape.89
  641.3 3.5 fusion.33
  644.8 153.2 %psum.7 = f32[2048]{0:T(1024)S(1)} all-reduce(f32[2048]{0:T(1024)S(1)} %get-tuple-element.3), channel_id=1, replica_groups=mesh['dp'=16,'expert'=64] {'dp','expert'}, use_global_device_ids=true, to_apply=%region_10.11 | all-reduce | flops 2048 | bytes 16384 | tf_op jit(solution)/shard_map/psum | solution.py:91
  798.1 0.6 add_multiply_fusion
  (16 shorter events, 0.2 us)
Async XLA Ops:
  7.2 157.1 %copy-start = (bf16[1024,32]{0,1:T(8,128)(2,1)S(1)}, bf16[1024,32]{0,1:T(8,128)(2,1)}, u32[]{:S(2)}) copy-start(bf16[1024,32]{0,1:T(8,128)(2,1)} %param.9) | copy-start | bytes 196612
  158.3 6.0 copy-start.3
  158.3 6.0 copy-start.1
  159.5 115.4 %all-to-all-start.1 = ((bf16[64,6,1024]{2,1,0:T(8,128)(2,1)}), bf16[64,6,1024]{2,1,0:T(8,128)(2,1)S(1)}, u32[]{:S(2)}, u32[]{:S(2)}) async-start(bf16[64,6,1024]{2,1,0:T(8,128)(2,1)} %reshape.85), calls=%async_computation.1 | async-start | bytes 2097152 | tf_op jit(solution)/shard_map/all_to_all | solution.py:59
  164.2 469.9 %all-gather.3.cloned.1.call-start = ((), (), s32[]{:S(2)}) async-start(), calls=%async_computation.2 | async-start | bytes 4198400 | tf_op jit(solution)/shard_map/all_gather | solution.py:84
  275.7 365.6 %copy-start.2 = (bf16[128,1024]{1,0:T(8,128)(2,1)}, bf16[128,1024]{1,0:T(8,128)(2,1)S(1)}, u32[]{:S(2)}) copy-start(bf16[128,1024]{1,0:T(8,128)(2,1)S(1)} %fusion.19) | copy-start | bytes 786436
Sparse Core Ops, SparseCore 0:
  277.2 356.8 all-gather.2
where the time goes:
time: 809 us; the launch traced here: 805 us
  waiting for transfers between devices  467 us (58%)
  blocking collectives  293 us (36%)
  between operations  14.2 us (2%)
  matrix products  12.4 us (2%)
  local copies, waits for them, and re-layouts  9.88 us (1%)
    all_gather x1, waiting for transfers between devices, per_device(): lax.all_gather(text_unit, ('dp', 'expert'), axis=0, tiled=True)  357 us
    psum x1, blocking collectives, per_device(): every_column = lax.psum(column_sums, ('dp', 'expert'))  153 us
    all_to_all x1, blocking collectives, per_device(): lax.all_to_all(doubled, 'expert', split_axis=0, concat_axis=0, tiled=True)  140 us
    all_to_all x1, waiting for transfers between devices, per_device(): lax.all_to_all(partial_value, 'expert', split_axis=0, concat_axis=0, tile...  110 us
  transfers between devices with their start and end apart: 2, of which 2 were waited for; matrix products, arithmetic and copies ran while one was open for 0% of the time, Pallas kernels for 0%

commit v1 on v0

v1 whole, which is shorter than its diff:
```python
import functools

import jax
import jax.numpy as jnp
from jax import lax
from jax.experimental import pallas as pl
from jax.experimental.pallas import tpu as pltpu
from jax.sharding import PartitionSpec as P

IMG_TOK = 48
LANES = 128
CORES = 2
logit_scale = 20.0
norm_eps = 1e-06
MESH = pl.DeviceIdType.MESH
bf16 = jnp.bfloat16
f32 = jnp.float32


def iota(shape, axis):
    return lax.broadcasted_iota(jnp.int32, shape, axis)


def dot(a, b):
    return jnp.dot(a, b, preferred_element_type=f32)


def dot_nt(a, b):
    return lax.dot_general(a, b, (((1,), (1,)), ((), ())), preferred_element_type=f32)


def chunk_major(blocks, chunks, rows):
    size = blocks * chunks * rows
    to = iota((size, 1), 0)
    chunk, rest = to // (blocks * rows), to % (blocks * rows)
    source = (rest // rows) * (chunks * rows) + chunk * rows + rest % rows
    return (iota((size, size), 1) == source).astype(bf16)


def block_major(blocks, chunks, rows):
    size = blocks * chunks * rows
    to = iota((size, 1), 0)
    block, rest = to // (chunks * rows), to % (chunks * rows)
    source = (rest // rows) * (blocks * rows) + block * rows + rest % rows
    return (iota((size, size), 1) == source).astype(bf16)


def kernel(
    cfg, tok, ids, clen, router_t, win_hbm, wout_hbm, out_ref, loss_ref,
    win, wout, unfold, fold, unfold_z, unfold_p, slot_col_ref, gate_ref,
    out_blocks, arrived, sib_arrived, x_rows, total,
    own_part, send_part, sib_part, ret_blocks, ret_arrived, token_total,
    units, image_blocks, text_blocks, image_rows, text_rows,
    row_vec, col_vec, row_parts, col_parts,
    w_sem, d_send, d_recv, f_send, f_recv, p_send, p_recv, r_send, r_recv,
    g_send, g_recv, s_send, s_recv,
):
    Z, DP, CAP, CH, GS, FFC = cfg
    PLANE = DP * CORES
    GROUPS = Z // GS
    BLK = CAP * CH
    ROWS = GS * CAP
    tokens = tok.shape[0]
    half = tokens // 2
    dp = lax.axis_index("dp")
    ex = lax.axis_index("expert")
    z = ex // CORES
    core = ex % CORES

    def ring(k):
        return {"dp": dp, "expert": lax.rem(z + k, Z) * CORES + core}

    def in_plane(m):
        return {
            "dp": lax.rem(dp + m // CORES, DP),
            "expert": z * CORES + lax.rem(core + m % CORES, CORES),
        }

    sibling = {"dp": dp, "expert": z * CORES + (1 - core)}

    def offset(q):
        return jnp.where(q % 2 == 1, Z // 2 - (q + 1) // 2, lax.rem(q // 2 + Z // 2, Z))

    barrier = pltpu.get_barrier_semaphore()

    def greet_ring(k, c):
        pl.semaphore_signal(barrier, inc=1, device_id=ring(k), device_id_type=MESH)
        return c

    def greet_plane(m, c):
        pl.semaphore_signal(barrier, inc=1, device_id=in_plane(m), device_id_type=MESH)
        return c

    lax.fori_loop(1, Z, greet_ring, 0)
    lax.fori_loop(1, PLANE, greet_plane, 0)

    load_in = pltpu.make_async_copy(win_hbm.at[0], win, w_sem.at[0])
    load_out = pltpu.make_async_copy(wout_hbm.at[0], wout, w_sem.at[1])
    load_in.start()
    load_out.start()

    unfold[...] = chunk_major(GS, CH, CAP)
    fold[...] = block_major(GS, CH, CAP)
    ids_row = jnp.concatenate([ids[0], ids[1]], axis=1)
    eye = iota((tokens, tokens), 0) == iota((tokens, tokens), 1)
    onehot_t = iota((Z, tokens), 0) == ids_row
    upto = (iota((tokens, tokens), 0) <= iota((tokens, tokens), 1)).astype(bf16)
    running = dot(onehot_t.astype(bf16), upto)
    position = jnp.sum(jnp.where(onehot_t, running, 0.0), axis=0, keepdims=True).astype(jnp.int32) - 1
    ahead = ids_row - z
    ahead = jnp.where(ahead < 0, ahead + Z, ahead)
    signed = jnp.where(ahead > Z // 2, ahead - Z, ahead)
    away = jnp.abs(signed)
    order = 2 * (Z // 2 - away) - jnp.where((signed >= 0) & (away < Z // 2), 1, 0)
    slot_row = order * CAP + position
    slot_col_ref[...] = jnp.sum(jnp.where(eye, slot_row.astype(f32), 0.0), axis=1, keepdims=True).astype(jnp.int32)
    ids_col = jnp.sum(jnp.where(eye, ids_row.astype(f32), 0.0), axis=1, keepdims=True).astype(jnp.int32)

    def pack(g, c):
        mask = (slot_row == g * ROWS + iota((ROWS, tokens), 0)).astype(bf16)
        rows = dot(mask, tok[...]).astype(bf16)
        stacked = jnp.concatenate([rows[:, j * LANES:(j + 1) * LANES] for j in range(CH)], axis=0)
        out_blocks[pl.ds(g * GS, GS)] = dot(fold[...], stacked).astype(bf16).reshape(GS, BLK, LANES)
        return c

    lax.fori_loop(0, GROUPS, pack, 0)

    pl.semaphore_wait(barrier, Z - 1 + PLANE - 1)

    def send_out(q, c):
        pltpu.make_async_remote_copy(
            src_ref=out_blocks.at[q], dst_ref=arrived.at[q], send_sem=d_send,
            recv_sem=d_recv.at[q // GS], device_id=ring(offset(q)), device_id_type=MESH,
        ).start()
        return c

    lax.fori_loop(0, Z - 1, send_out, 0)
    pltpu.make_async_copy(out_blocks.at[Z - 1], arrived.at[Z - 1], d_recv.at[GROUPS - 1]).start()

    logits = dot_nt(tok[...], router_t[...])
    onehot = iota((tokens, Z), 1) == ids_col
    gate_ref[...] = jax.nn.sigmoid(jnp.sum(jnp.where(onehot, logits, 0.0), axis=1, keepdims=True))
    token_total[...] = jnp.zeros_like(token_total)
    unfold_z[...] = chunk_major(Z, CH, 2)
    unfold_p[...] = chunk_major(PLANE, CH, 2)
    load_in.wait()
    load_out.wait()

    def group(ref, g):
        return ref.at[pl.ds(g * GS, GS)]

    def unpack(ref, g, base):
        blocks = ref[pl.ds(g * GS, GS)].reshape(GS * BLK, LANES)
        rows = dot(unfold[...], blocks).astype(bf16)
        for j in range(CH):
            x_rows[base:base + ROWS, j * LANES:(j + 1) * LANES] = rows[j * ROWS:(j + 1) * ROWS]

    def forward(g):
        return pltpu.make_async_remote_copy(
            src_ref=group(arrived, g), dst_ref=group(sib_arrived, g), send_sem=f_send.at[g],
            recv_sem=f_recv.at[g], device_id=sibling, device_id_type=MESH,
        )

    def swap(g):
        return pltpu.make_async_remote_copy(
            src_ref=send_part.at[g], dst_ref=sib_part.at[g], send_sem=p_send.at[g],
            recv_sem=p_recv.at[g], device_id=sibling, device_id_type=MESH,
        )

    def finish(g):
        swap(g).wait_recv()
        both = (own_part[g].astype(f32) + sib_part[g].astype(f32)).astype(bf16)
        stacked = jnp.concatenate([both[:, j * LANES:(j + 1) * LANES] for j in range(CH)], axis=0)
        ret_blocks[pl.ds(g * GS, GS)] = dot(fold[...], stacked).astype(bf16).reshape(GS, BLK, LANES)

        def send_back(i, c):
            q = g * GS + i
            pltpu.make_async_remote_copy(
                src_ref=ret_blocks.at[q], dst_ref=ret_arrived.at[q], send_sem=r_send,
                recv_sem=r_recv.at[g], device_id=ring(Z - offset(q)), device_id_type=MESH,
            ).start()
            return c

        lax.fori_loop(0, jnp.where(g == GROUPS - 1, GS - 1, GS), send_back, 0)

        @pl.when(g == GROUPS - 1)
        def _():
            pltpu.make_async_copy(ret_blocks.at[Z - 1], ret_arrived.at[Z - 1], r_recv.at[g]).start()

    def work(g, c):
        pltpu.make_async_copy(group(arrived, g), group(arrived, g), d_recv.at[g]).wait()
        forward(g).start()
        unpack(arrived, g, 0)

        @pl.when(g > 0)
        def _():
            finish(g - 1)

        forward(g).wait_recv()
        unpack(sib_arrived, g, ROWS)
        total[...] = jnp.zeros_like(total)

        def hidden_chunk(i, c):
            cols = pl.ds(pl.multiple_of(i * FFC, FFC), FFC)
            hidden = jax.nn.gelu(dot(x_rows[...], win[:, cols])).astype(bf16)
            total[...] += dot(hidden, wout[cols, :])
            return c

        lax.fori_loop(0, win.shape[1] // FFC, hidden_chunk, 0)
        own_part[g] = total[0:ROWS].astype(bf16)
        send_part[g] = total[ROWS:2 * ROWS].astype(bf16)
        swap(g).start()
        return c

    lax.fori_loop(0, GROUPS, work, 0)
    finish(GROUPS - 1)

    def collect(g, c):
        pltpu.make_async_copy(group(ret_arrived, g), group(ret_arrived, g), r_recv.at[g]).wait()
        unpack(ret_arrived, g, 0)
        mask = (slot_col_ref[...] == g * ROWS + iota((tokens, ROWS), 1)).astype(bf16)
        token_total[...] += dot(mask, x_rows[0:ROWS])
        return c

    lax.fori_loop(0, GROUPS, collect, 0)

    layer_out = (tok[...].astype(f32) + gate_ref[...] * token_total[...]).astype(bf16)
    out_ref[...] = layer_out

    UR = 16
    row, at = iota((UR, tokens), 0), iota((UR, tokens), 1)
    first = jnp.where((row == 0) | (row == 2), 0, half)
    length = jnp.where(row == 2, clen[0], clen[1])
    start = jnp.where(row < 2, first, first + IMG_TOK)
    stop = first + IMG_TOK + jnp.where(row < 2, 0, length)
    pool = ((at >= start) & (at < stop) & (row < 4)).astype(bf16)
    row1 = iota((UR, 1), 0)
    count = jnp.where(row1 < 2, IMG_TOK, jnp.where(row1 == 2, clen[0], clen[1])).astype(f32)
    vectors = dot(pool, layer_out) / count
    squares = jnp.sum(vectors * vectors, axis=1, keepdims=True) + norm_eps
    unit = (vectors * lax.rsqrt(squares)).astype(bf16)
    gram = logit_scale * dot_nt(unit, unit)
    gram_row, gram_col = iota((UR, UR), 0), iota((UR, UR), 1)

    def pick(i):
        hit = (gram_row == i) & (gram_col == i + 2)
        return jnp.sum(jnp.sum(jnp.where(hit, gram, 0.0), axis=1, keepdims=True), axis=0, keepdims=True)

    stacked = jnp.concatenate([unit[:, j * LANES:(j + 1) * LANES] for j in range(CH)], axis=0)
    to = iota((2 * UR, 1), 0)
    inner = to % (2 * CH)
    source = (inner // 2) * UR + (to // (2 * CH)) * 2 + inner % 2
    select = (iota((2 * UR, CH * UR), 1) == source).astype(bf16)
    packed = dot(select, stacked).astype(bf16)
    units[0] = packed[0:UR]
    units[1] = packed[UR:2 * UR]

    def send_images(q, c):
        pltpu.make_async_remote_copy(
            src_ref=units.at[0], dst_ref=image_blocks.at[q], send_sem=g_send.at[0],
            recv_sem=g_recv.at[0], device_id=ring(offset(q)), device_id_type=MESH,
        ).start()
        return c

    def send_texts(m, c):
        pltpu.make_async_remote_copy(
            src_ref=units.at[1], dst_ref=text_blocks.at[m], send_sem=g_send.at[1],
            recv_sem=g_recv.at[1], device_id=in_plane(m), device_id_type=MESH,
        ).start()
        return c

    lax.fori_loop(0, Z - 1, send_images, 0)
    lax.fori_loop(1, PLANE, send_texts, 0)
    image_blocks[Z - 1] = packed[0:UR]
    text_blocks[0] = packed[UR:2 * UR]
    row_vec[...] = jnp.zeros_like(row_vec)
    col_vec[...] = jnp.zeros_like(col_vec)

    def others(ref, first, sem):
        part = ref.at[pl.ds(first, ref.shape[0] - 1)]
        return pltpu.make_async_copy(part, part, sem)

    def lay_rows(blocks, matrix, rows_ref, n):
        rows = dot(matrix[...], blocks[...].reshape(n * UR, LANES)).astype(bf16)
        for j in range(CH):
            rows_ref[:, j * LANES:(j + 1) * LANES] = rows[j * 2 * n:(j + 1) * 2 * n]

    others(text_blocks, 1, g_recv.at[1]).wait()
    lay_rows(text_blocks, unfold_p, text_rows, PLANE)
    others(image_blocks, 0, g_recv.at[0]).wait()
    lay_rows(image_blocks, unfold_z, image_rows, Z)
    by_image = jnp.exp(logit_scale * dot_nt(text_rows[...], image_rows[...]))
    row_vec[:, 0:2 * Z] = jnp.sum(by_image, axis=0, keepdims=True)
    by_text = jnp.exp(logit_scale * dot_nt(image_rows[...], text_rows[...]))
    col_vec[:, 0:2 * PLANE] = jnp.sum(by_text, axis=0, keepdims=True)

    def send_rows(q, c):
        pltpu.make_async_remote_copy(
            src_ref=row_vec, dst_ref=row_parts.at[q], send_sem=s_send.at[0],
            recv_sem=s_recv.at[0], device_id=ring(offset(q)), device_id_type=MESH,
        ).start()
        return c

    def send_cols(m, c):
        pltpu.make_async_remote_copy(
            src_ref=col_vec, dst_ref=col_parts.at[m], send_sem=s_send.at[1],
            recv_sem=s_recv.at[1], device_id=in_plane(m), device_id_type=MESH,
        ).start()
        return c

    lax.fori_loop(0, Z - 1, send_rows, 0)
    lax.fori_loop(1, PLANE, send_cols, 0)
    row_parts[Z - 1] = row_vec[...]
    col_parts[0] = col_vec[...]

    q = iota((Z, 1, LANES), 0)
    lane = iota((Z, 1, LANES), 2)
    back = jnp.where((q == 0) | (q == Z - 1), q, jnp.where(q % 2 == 1, q + 1, q - 1))
    m = iota((PLANE, 1, LANES), 0)
    mlane = iota((PLANE, 1, LANES), 2)
    mback = ((DP - m // CORES) % DP) * CORES + ((CORES - m % CORES) % CORES)

    def mine(parts, lanes, at):
        kept = jnp.where(lanes == at, parts, 0.0)
        return jnp.sum(jnp.sum(kept, axis=0), axis=1, keepdims=True)

    others(col_parts, 1, s_recv.at[1]).wait()
    col_total = [mine(col_parts[...], mlane, 2 * mback + i) for i in range(2)]
    others(row_parts, 0, s_recv.at[0]).wait()
    row_total = [mine(row_parts[...], lane, 2 * back + i) for i in range(2)]
    losses = [
        0.5 * (jnp.log(row_total[i]) - pick(i)) + 0.5 * (jnp.log(col_total[i]) - pick(i))
        for i in range(2)
    ]
    loss_ref[...] = jnp.where(iota((1, LANES), 1) == 0, losses[0], losses[1])

    def sent(part, sem):
        pltpu.make_async_copy(part, part, sem).wait()

    sent(out_blocks.at[pl.ds(0, Z - 1)], d_send)
    sent(ret_blocks.at[pl.ds(0, Z - 1)], r_send)

    def drain(g, c):
        forward(g).wait_send()
        swap(g).wait_send()
        return c

    lax.fori_loop(0, GROUPS, drain, 0)
    sent(image_blocks.at[pl.ds(0, Z - 1)], g_send.at[0])
    sent(text_blocks.at[pl.ds(1, PLANE - 1)], g_send.at[1])
    sent(row_parts.at[pl.ds(0, Z - 1)], s_send.at[0])
    sent(col_parts.at[pl.ds(1, PLANE - 1)], s_send.at[1])


def per_device(tokens, expert_ids, caption_len, router, expert_in, expert_out, *, cfg):
    pairs, seq, width = tokens.shape
    count = pairs * seq
    Z, DP, CAP, CH, GS, FFC = cfg
    PLANE = DP * CORES
    GROUPS = Z // GS
    BLK = CAP * CH
    ROWS = GS * CAP
    hidden = expert_in.shape[2]
    vmem = pl.BlockSpec(memory_space=pltpu.VMEM)
    dma = pltpu.SemaphoreType.DMA
    blocks = pltpu.VMEM((Z, BLK, LANES), bf16)
    parts = pltpu.VMEM((GROUPS, ROWS, width), bf16)
    out, loss = pl.pallas_call(
        functools.partial(kernel, cfg),
        out_shape=(
            jax.ShapeDtypeStruct((count, width), bf16),
            jax.ShapeDtypeStruct((1, LANES), f32),
        ),
        in_specs=[
            vmem, vmem, pl.BlockSpec(memory_space=pltpu.SMEM), vmem,
            pl.BlockSpec(memory_space=pl.ANY), pl.BlockSpec(memory_space=pl.ANY),
        ],
        out_specs=(vmem, vmem),
        scratch_shapes=[
            pltpu.VMEM((width, hidden), bf16),
            pltpu.VMEM((hidden, width), bf16),
            pltpu.VMEM((GS * BLK, GS * BLK), bf16),
            pltpu.VMEM((GS * BLK, GS * BLK), bf16),
            pltpu.VMEM((Z * 16, Z * 16), bf16),
            pltpu.VMEM((PLANE * 16, PLANE * 16), bf16),
            pltpu.VMEM((count, 1), jnp.int32),
            pltpu.VMEM((count, 1), f32),
            blocks, blocks, blocks,
            pltpu.VMEM((2 * ROWS, width), bf16),
            pltpu.VMEM((2 * ROWS, width), f32),
            parts, parts, parts, blocks, blocks,
            pltpu.VMEM((count, width), f32),
            pltpu.VMEM((2, 16, LANES), bf16),
            pltpu.VMEM((Z, 16, LANES), bf16),
            pltpu.VMEM((PLANE, 16, LANES), bf16),
            pltpu.VMEM((2 * Z, width), bf16),
            pltpu.VMEM((2 * PLANE, width), bf16),
            pltpu.VMEM((1, LANES), f32),
            pltpu.VMEM((1, LANES), f32),
            pltpu.VMEM((Z, 1, LANES), f32),
            pltpu.VMEM((PLANE, 1, LANES), f32),
            dma((2,)), dma, dma((GROUPS,)), dma((GROUPS,)), dma((GROUPS,)),
            dma((GROUPS,)), dma((GROUPS,)), dma, dma((GROUPS,)),
            dma((2,)), dma((2,)), dma((2,)), dma((2,)),
        ],
        compiler_params=pltpu.CompilerParams(
            collective_id=0, has_side_effects=True, vmem_limit_bytes=40 << 20
        ),
        cost_estimate=pl.CostEstimate(
            flops=8 * Z * CAP * width * hidden, bytes_accessed=4 * width * hidden, transcendentals=0
        ),
        name="expert_contrast",
    )(
        tokens.reshape(count, width),
        jnp.swapaxes(expert_ids, 1, 2),
        caption_len,
        router.T,
        expert_in,
        expert_out,
    )
    return out.reshape(pairs, seq, width), loss[0, :pairs]


def solution(mesh, cap=6, group=8, ff_chunk=512):
    cfg = (mesh.shape["expert"] // CORES, mesh.shape["dp"], cap, 8, group, ff_chunk)
    return jax.shard_map(
        functools.partial(per_device, cfg=cfg),
        mesh=mesh,
        in_specs=(
            P(("dp", "expert"), None, None),
            P(("dp", "expert"), None, None),
            P(("dp", "expert")),
            P(),
            P("expert", None, None),
            P("expert", None, None),
        ),
        out_specs=(P(("dp", "expert"), None, None), P(("dp", "expert"))),
        check_vma=False,
    )
```

time: 809 us -> 137 us (0.17)
  waiting for transfers between devices: 467 us -> 0 us
  blocking collectives: 293 us -> 0 us
  Pallas kernels: 0 us -> 128 us
  between operations: 14.2 us -> 0.65 us
  matrix products: 12.4 us -> 0 us
    all_gather x1 -> x0, waiting for transfers between devices: 357 us -> none  [per_device(): lax.all_gather(text_unit, ('dp', 'expert'), axis=0, tiled=True)]
    psum x1 -> x0, blocking collectives: 153 us -> none  [per_device(): every_column = lax.psum(column_sums, ('dp', 'expert'))]
    all_to_all x1 -> x0, blocking collectives: 140 us -> none  [per_device(): lax.all_to_all(doubled, 'expert', split_axis=0, concat_axis=0, tiled=True)]
    pallas_call x0 -> x1, Pallas kernels: none -> 128 us  [per_device(): pl.pallas_call(functools.partial(kernel, cfg), out_shape=(jax.ShapeDtypeS...]
    all_to_all x1 -> x0, waiting for transfers between devices: 110 us -> none  [per_device(): lax.all_to_all(partial_value, 'expert', split_axis=0, concat_axis=0, tile...]
    dot_general x5 -> x0, matrix products: 12.4 us -> none  [the longest x1 7.05 us: partial_value(): jnp.dot(hidden, second_layer, preferred_element_type=jnp.float32)]
  transfers between devices with their start and end apart: 2 -> 0, of which waited for: 2 -> 0; matrix products, arithmetic and copies ran while one was open for 0% -> 0% of each run, Pallas kernels for 0% -> 0%
where the time goes in v1:
time: 137 us
  Pallas kernels  128 us (93%)
  local copies, waits for them, and re-layouts  8.71 us (6%)
    pallas_call x1, Pallas kernels, per_device(): pl.pallas_call(functools.partial(kernel, cfg), out_shape=(jax.ShapeDtypeS...  128 us
    unnamed x13, local copies, waits for them, and re-layouts  8.19 us

profile of v1, /device:TPU:6, one launch (start us, length us, event | category | flops | bytes accessed | tf_op | source)
XLA Modules:
  0.0 137.2 jit_solution(2765588915406394580)
XLA Ops:
  0.6 0.0 copy-start
  0.6 2.2 %copy-done = bf16[1,1024,2048]{2,1,0:T(8,128)(2,1)S(1)} copy-done((bf16[1,1024,2048]{2,1,0:T(8,128)(2,1)S(1)}, bf16[1,1024,2048]{2,1,0:T(8,128)(2,1)}, u32[]{:S(2)}) %copy-start) | copy-done | bytes 4194328
  2.8 0.0 copy-start.1
  2.8 2.2 %copy-done.1 = bf16[1,2048,1024]{2,1,0:T(8,128)(2,1)S(1)} copy-done((bf16[1,2048,1024]{2,1,0:T(8,128)(2,1)S(1)}, bf16[1,2048,1024]{2,1,0:T(8,128)(2,1)}, u32[]{:S(2)}) %copy-start.1) | copy-done | bytes 4194328
  5.0 0.0 copy-start.2
  5.0 0.9 copy-done.2
  6.0 0.0 copy-start.3
  6.0 0.8 copy-done.3
  6.8 0.0 copy-start.4
  6.8 0.7 copy-done.4
  7.5 0.0 copy-start.5
  7.5 0.7 copy-done.5
  8.1 127.8 %expert_contrast.1 = (bf16[128,1024]{1,0:T(8,128)(2,1)S(1)}, f32[1,128]{1,0:T(1,128)S(1)}) custom-call(bf16[128,1024]{1,0:T(8,128)(2,1)S(1)} %bitcast.9, s32[2,1,64]{2,1,0:T(1,128)S(1)} %bitcast.11, s32[2]{0:T(128)S(1)} %copy-done.5, bf16[32,1024]{1,0:T(8,128)(2,1)S(1)} %bitcast.10, bf16[1,1024,2048]{2,1,0:T(8,128)(2,1)S(1)} %copy-done, ...), custom_call_target="tpu_custom_call" | custom-call | flops 3221225472 | bytes 8388608 | tf_op jit(solution)/shard_map/expert_contrast/pallas_call | solution.py:368
  136.0 0.5 slice_bitcast_fusion
  136.5 0.7 copy.10
Async XLA Ops:
  0.6 2.2 %copy-start = (bf16[1,1024,2048]{2,1,0:T(8,128)(2,1)S(1)}, bf16[1,1024,2048]{2,1,0:T(8,128)(2,1)}, u32[]{:S(2)}) copy-start(bf16[1,1024,2048]{2,1,0:T(8,128)(2,1)} %win_hbm.1) | copy-start | bytes 12582916
  2.8 2.2 %copy-start.1 = (bf16[1,2048,1024]{2,1,0:T(8,128)(2,1)S(1)}, bf16[1,2048,1024]{2,1,0:T(8,128)(2,1)}, u32[]{:S(2)}) copy-start(bf16[1,2048,1024]{2,1,0:T(8,128)(2,1)} %wout_hbm.1) | copy-start | bytes 12582916
  5.0 0.9 copy-start.2
  6.0 0.8 copy-start.3
  6.8 0.7 copy-start.4
  7.5 0.7 copy-start.5

commit v2 on v1

--- a/solution.py
+++ b/solution.py
@@ -46,13 +46,13 @@
 
 
 def kernel(
-    cfg, tok, ids, clen, router_t, win_hbm, wout_hbm, out_ref, loss_ref,
-    win, wout, unfold, fold, unfold_z, unfold_p, slot_col_ref, gate_ref,
+    cfg, tok_hbm, ids_hbm, clen_hbm, router_hbm, win_hbm, wout_hbm, out_hbm, loss_ref,
+    tok, ids, clen, router_t, out_ref, win, wout, unfold, fold, unfold_z, unfold_p, slot_col_ref, gate_ref,
     out_blocks, arrived, sib_arrived, x_rows, total,
     own_part, send_part, sib_part, ret_blocks, ret_arrived, token_total,
     units, image_blocks, text_blocks, image_rows, text_rows,
     row_vec, col_vec, row_parts, col_parts,
-    w_sem, d_send, d_recv, f_send, f_recv, p_send, p_recv, r_send, r_recv,
+    w_sem, far_sem, d_send, d_recv, f_send, f_recv, p_send, p_recv, r_send, r_recv,
     g_send, g_recv, s_send, s_recv,
 ):
     Z, DP, CAP, CH, GS, FFC = cfg
@@ -91,16 +91,25 @@
         pl.semaphore_signal(barrier, inc=1, device_id=in_plane(m), device_id_type=MESH)
         return c
 
-    lax.fori_loop(1, Z, greet_ring, 0)
+    NEAR = Z // 4
+    load_ids = pltpu.make_async_copy(ids_hbm, ids, w_sem.at[0])
+    load_tok = pltpu.make_async_copy(tok_hbm, tok, w_sem.at[1])
+    load_router = pltpu.make_async_copy(router_hbm, router_t, w_sem.at[2])
+    load_clen = pltpu.make_async_copy(clen_hbm, clen, w_sem.at[3])
+    load_in = pltpu.make_async_copy(win_hbm.at[0], win, w_sem.at[4])
+    load_out = pltpu.make_async_copy(wout_hbm.at[0], wout, w_sem.at[5])
+    load_ids.start()
+    load_tok.start()
+    lax.fori_loop(1, NEAR + 1, greet_ring, 0)
+    lax.fori_loop(Z - NEAR, Z, greet_ring, 0)
     lax.fori_loop(1, PLANE, greet_plane, 0)
-
-    load_in = pltpu.make_async_copy(win_hbm.at[0], win, w_sem.at[0])
-    load_out = pltpu.make_async_copy(wout_hbm.at[0], wout, w_sem.at[1])
+    load_router.start()
+    load_clen.start()
     load_in.start()
     load_out.start()
 
-    unfold[...] = chunk_major(GS, CH, CAP)
     fold[...] = block_major(GS, CH, CAP)
+    load_ids.wait()
     ids_row = jnp.concatenate([ids[0], ids[1]], axis=1)
     eye = iota((tokens, tokens), 0) == iota((tokens, tokens), 1)
     onehot_t = iota((Z, tokens), 0) == ids_row
@@ -116,7 +125,10 @@
     slot_col_ref[...] = jnp.sum(jnp.where(eye, slot_row.astype(f32), 0.0), axis=1, keepdims=True).astype(jnp.int32)
     ids_col = jnp.sum(jnp.where(eye, ids_row.astype(f32), 0.0), axis=1, keepdims=True).astype(jnp.int32)
 
-    def pack(g, c):
+    load_tok.wait()
+
+    def pack(i, c):
+        g = GROUPS - 1 - i
         mask = (slot_row == g * ROWS + iota((ROWS, tokens), 0)).astype(bf16)
         rows = dot(mask, tok[...]).astype(bf16)
         stacked = jnp.concatenate([rows[:, j * LANES:(j + 1) * LANES] for j in range(CH)], axis=0)
@@ -124,8 +136,6 @@
         return c
 
     lax.fori_loop(0, GROUPS, pack, 0)
-
-    pl.semaphore_wait(barrier, Z - 1 + PLANE - 1)
 
     def send_out(q, c):
         pltpu.make_async_remote_copy(
@@ -134,9 +144,17 @@
         ).start()
         return c
 
-    lax.fori_loop(0, Z - 1, send_out, 0)
+    pl.semaphore_wait(barrier, 2 * NEAR + PLANE - 1)
+    for end in (NEAR, Z - NEAR):
+        pl.semaphore_signal(far_sem, inc=1, device_id=ring(end), device_id_type=MESH)
+    lax.fori_loop(Z // 2 - 1, Z - 1, send_out, 0)
     pltpu.make_async_copy(out_blocks.at[Z - 1], arrived.at[Z - 1], d_recv.at[GROUPS - 1]).start()
-
+    unfold[...] = chunk_major(GS, CH, CAP)
+    pl.semaphore_wait(far_sem, 2)
+    lax.fori_loop(0, Z // 2 - 1, send_out, 0)
+
+    load_router.wait()
+    load_clen.wait()
     logits = dot_nt(tok[...], router_t[...])
     onehot = iota((tokens, Z), 1) == ids_col
     gate_ref[...] = jax.nn.sigmoid(jnp.sum(jnp.where(onehot, logits, 0.0), axis=1, keepdims=True))
@@ -173,6 +191,7 @@
         stacked = jnp.concatenate([both[:, j * LANES:(j + 1) * LANES] for j in range(CH)], axis=0)
         ret_blocks[pl.ds(g * GS, GS)] = dot(fold[...], stacked).astype(bf16).reshape(GS, BLK, LANES)
 
+    def send_group(g):
         def send_back(i, c):
             q = g * GS + i
             pltpu.make_async_remote_copy(
@@ -187,14 +206,22 @@
         def _():
             pltpu.make_async_copy(ret_blocks.at[Z - 1], ret_arrived.at[Z - 1], r_recv.at[g]).start()
 
-    def work(g, c):
+    def place(i):
+        return jnp.where(i < GROUPS // 2, GROUPS - 1 - i, i - GROUPS // 2)
+
+    def work(i, c):
+        g = place(i)
         pltpu.make_async_copy(group(arrived, g), group(arrived, g), d_recv.at[g]).wait()
         forward(g).start()
         unpack(arrived, g, 0)
 
-        @pl.when(g > 0)
+        @pl.when(i > 0)
         def _():
-            finish(g - 1)
+            finish(place(i - 1))
+
+        @pl.when(i > GROUPS // 2)
+        def _():
+            send_group(place(i - 1))
 
         forward(g).wait_recv()
         unpack(sib_arrived, g, ROWS)
@@ -213,7 +240,13 @@
         return c
 
     lax.fori_loop(0, GROUPS, work, 0)
-    finish(GROUPS - 1)
+    finish(GROUPS // 2 - 1)
+
+    def send_rest(g, c):
+        send_group(g)
+        return c
+
+    lax.fori_loop(GROUPS // 2 - 1, GROUPS, send_rest, 0)
 
     def collect(g, c):
         pltpu.make_async_copy(group(ret_arrived, g), group(ret_arrived, g), r_recv.at[g]).wait()
@@ -226,6 +259,8 @@
 
     layer_out = (tok[...].astype(f32) + gate_ref[...] * token_total[...]).astype(bf16)
     out_ref[...] = layer_out
+    store = pltpu.make_async_copy(out_ref, out_hbm, w_sem.at[0])
+    store.start()
 
     UR = 16
     row, at = iota((UR, tokens), 0), iota((UR, tokens), 1)
@@ -334,6 +369,7 @@
     ]
     loss_ref[...] = jnp.where(iota((1, LANES), 1) == 0, losses[0], losses[1])
 
+    store.wait()
     def sent(part, sem):
         pltpu.make_async_copy(part, part, sem).wait()
 
@@ -362,6 +398,7 @@
     ROWS = GS * CAP
     hidden = expert_in.shape[2]
     vmem = pl.BlockSpec(memory_space=pltpu.VMEM)
+    hbm = pl.BlockSpec(memory_space=pltpu.HBM)
     dma = pltpu.SemaphoreType.DMA
     blocks = pltpu.VMEM((Z, BLK, LANES), bf16)
     parts = pltpu.VMEM((GROUPS, ROWS, width), bf16)
@@ -372,11 +409,15 @@
             jax.ShapeDtypeStruct((1, LANES), f32),
         ),
         in_specs=[
-            vmem, vmem, pl.BlockSpec(memory_space=pltpu.SMEM), vmem,
-            pl.BlockSpec(memory_space=pl.ANY), pl.BlockSpec(memory_space=pl.ANY),
+            hbm, hbm, hbm, hbm, hbm, hbm,
         ],
-        out_specs=(vmem, vmem),
+        out_specs=(hbm, vmem),
         scratch_shapes=[
+            pltpu.VMEM((count, width), bf16),
+            pltpu.VMEM((pairs, 1, seq), jnp.int32),
+            pltpu.SMEM((pairs,), jnp.int32),
+            pltpu.VMEM((Z, width), bf16),
+            pltpu.VMEM((count, width), bf16),
             pltpu.VMEM((width, hidden), bf16),
             pltpu.VMEM((hidden, width), bf16),
             pltpu.VMEM((GS * BLK, GS * BLK), bf16),
@@ -399,12 +440,12 @@
             pltpu.VMEM((1, LANES), f32),
             pltpu.VMEM((Z, 1, LANES), f32),
             pltpu.VMEM((PLANE, 1, LANES), f32),
-            dma((2,)), dma, dma((GROUPS,)), dma((GROUPS,)), dma((GROUPS,)),
+            dma((6,)), pltpu.SemaphoreType.REGULAR, dma, dma((GROUPS,)), dma((GROUPS,)), dma((GROUPS,)),
             dma((GROUPS,)), dma((GROUPS,)), dma, dma((GROUPS,)),
             dma((2,)), dma((2,)), dma((2,)), dma((2,)),
         ],
         compiler_params=pltpu.CompilerParams(
-            collective_id=0, has_side_effects=True, vmem_limit_bytes=40 << 20
+            collective_id=0, has_side_effects=True, vmem_limit_bytes=64 << 20
         ),
         cost_estimate=pl.CostEstimate(
             flops=8 * Z * CAP * width * hidden, bytes_accessed=4 * width * hidden, transcendentals=0

time: 137 us -> 135 us (0.985)
  local copies, waits for them, and re-layouts: 8.71 us -> 2.8 us
  Pallas kernels: 128 us -> 131 us
    unnamed x13 -> x1, local copies, waits for them, and re-layouts: 8.19 us -> 1.67 us
    pallas_call x1, Pallas kernels: 128 us -> 131 us  [per_device(): pl.pallas_call(functools.partial(kernel, cfg), out_shape=(jax.ShapeDtypeS...]
where the time goes in v2:
time: 135 us; the launch traced here: 134 us
  Pallas kernels  131 us (97%)
  local copies, waits for them, and re-layouts  2.8 us (2%)
    pallas_call x1, Pallas kernels, per_device(): pl.pallas_call(functools.partial(kernel, cfg), out_shape=(jax.ShapeDtypeS...  131 us

profile of v2, /device:TPU:6, one launch (start us, length us, event | category | flops | bytes accessed | tf_op | source)
XLA Modules:
  0.0 134.0 jit_solution(4700643944022761384)
XLA Ops:
  0.6 130.6 %expert_contrast.1 = (bf16[128,1024]{1,0:T(8,128)(2,1)}, f32[1,128]{1,0:T(1,128)}) custom-call(bf16[128,1024]{1,0:T(8,128)(2,1)} %bitcast.9, s32[2,1,64]{2,1,0:T(1,128)} %bitcast.11, s32[2]{0:T(128)} %clen_hbm.1, bf16[32,1024]{1,0:T(8,128)(2,1)} %bitcast.10, bf16[1,1024,2048]{2,1,0:T(8,128)(2,1)} %win_hbm.1, bf16[1,2048,1024]{2,1,0:T(8,128)(2,1)} %wout_hbm.1), custom_call_target="tpu_custom_call" | custom-call | flops 3221225472 | bytes 8388608 | tf_op jit(solution)/shard_map/expert_contrast/pallas_call | solution.py:405
  131.2 1.1 slice_bitcast_fusion
  132.4 1.7 %copy.10 = bf16[2,64,1024]{2,1,0:T(8,128)(2,1)} copy(bf16[2,64,1024]{2,1,0:T(8,128)(2,1)} %bitcast.8) | data formatting | bytes 524288

commit v3 on v2

--- a/solution.py
+++ b/solution.py
@@ -45,21 +45,58 @@
     return (iota((size, size), 1) == source).astype(bf16)
 
 
+def plane_shape(DP):
+    XN = 1
+    while 4 * XN * XN <= DP:
+        XN *= 2
+    return XN, DP // XN
+
+
+def meeting(Z):
+    if Z % 32:
+        return Z, 1, []
+    images, captions = 8, 5
+    seen, repeated = set(), []
+    for i in range(images):
+        for j in range(captions):
+            apart = (image_offset(Z, i) - caption_offset(Z, j)) % Z
+            if apart in seen:
+                repeated.append((i, j))
+            seen.add(apart)
+    assert len(seen) == Z
+    return images, captions, repeated
+
+
+def image_offset(Z, i):
+    if Z % 32:
+        return i
+    return (Z // 4 - i // 2) * (1 - 2 * (i % 2))
+
+
+def caption_offset(Z, j):
+    if Z % 32:
+        return 0 * j
+    size = Z // 4 - (j - 1) // 2 * (Z // 8)
+    return (1 - (j == 0)) * size * (1 - 2 * (j % 2))
+
+
 def kernel(
     cfg, tok_hbm, ids_hbm, clen_hbm, router_hbm, win_hbm, wout_hbm, out_hbm, loss_ref,
     tok, ids, clen, router_t, out_ref, win, wout, unfold, fold, unfold_z, unfold_p, slot_col_ref, gate_ref,
     out_blocks, arrived, sib_arrived, x_rows, total,
     own_part, send_part, sib_part, ret_blocks, ret_arrived, token_total,
-    units, image_blocks, text_blocks, image_rows, text_rows,
+    units, image_blocks, text_blocks, image_rows, text_rows, once,
     row_vec, col_vec, row_parts, col_parts,
     w_sem, far_sem, d_send, d_recv, f_send, f_recv, p_send, p_recv, r_send, r_recv,
-    g_send, g_recv, s_send, s_recv,
+    g_send, g_recv, h_send, h_recv, s_send, s_recv,
 ):
     Z, DP, CAP, CH, GS, FFC = cfg
-    PLANE = DP * CORES
+    XN, YN = plane_shape(DP)
     GROUPS = Z // GS
     BLK = CAP * CH
     ROWS = GS * CAP
+    NA, NB, repeated = meeting(Z)
+    NI, NT = XN * NA, YN * CORES * NB
     tokens = tok.shape[0]
     half = tokens // 2
     dp = lax.axis_index("dp")
@@ -70,10 +107,18 @@
     def ring(k):
         return {"dp": dp, "expert": lax.rem(z + k, Z) * CORES + core}
 
-    def in_plane(m):
+    x, y = dp // YN, dp % YN
+
+    def along_x(dx, dz=0):
         return {
-            "dp": lax.rem(dp + m // CORES, DP),
-            "expert": z * CORES + lax.rem(core + m % CORES, CORES),
+            "dp": lax.rem(x + dx, XN) * YN + y,
+            "expert": lax.rem(z + dz + Z, Z) * CORES + core,
+        }
+
+    def along_y(m, dz=0):
+        return {
+            "dp": x * YN + lax.rem(y + m // CORES, YN),
+            "expert": lax.rem(z + dz + Z, Z) * CORES + lax.rem(core + m % CORES, CORES),
         }
 
     sibling = {"dp": dp, "expert": z * CORES + (1 - core)}
@@ -87,11 +132,15 @@
         pl.semaphore_signal(barrier, inc=1, device_id=ring(k), device_id_type=MESH)
         return c
 
-    def greet_plane(m, c):
-        pl.semaphore_signal(barrier, inc=1, device_id=in_plane(m), device_id_type=MESH)
-        return c
-
-    NEAR = Z // 4
+    def greet_x(m, c):
+        pl.semaphore_signal(barrier, inc=1, device_id=along_x(m), device_id_type=MESH)
+        return c
+
+    def greet_y(m, c):
+        pl.semaphore_signal(barrier, inc=1, device_id=along_y(m), device_id_type=MESH)
+        return c
+
+    NEAR = Z // 8
     load_ids = pltpu.make_async_copy(ids_hbm, ids, w_sem.at[0])
     load_tok = pltpu.make_async_copy(tok_hbm, tok, w_sem.at[1])
     load_router = pltpu.make_async_copy(router_hbm, router_t, w_sem.at[2])
@@ -102,7 +151,8 @@
     load_tok.start()
     lax.fori_loop(1, NEAR + 1, greet_ring, 0)
     lax.fori_loop(Z - NEAR, Z, greet_ring, 0)
-    lax.fori_loop(1, PLANE, greet_plane, 0)
+    lax.fori_loop(1, XN, greet_x, 0)
+    lax.fori_loop(1, YN * CORES, greet_y, 0)
     load_router.start()
     load_clen.start()
     load_in.start()
@@ -139,19 +189,25 @@
 
     def send_out(q, c):
         pltpu.make_async_remote_copy(
-            src_ref=out_blocks.at[q], dst_ref=arrived.at[q], send_sem=d_send,
+            src_ref=out_blocks.at[q], dst_ref=arrived.at[q], send_sem=d_send.at[q // GS],
             recv_sem=d_recv.at[q // GS], device_id=ring(offset(q)), device_id_type=MESH,
         ).start()
         return c
 
-    pl.semaphore_wait(barrier, 2 * NEAR + PLANE - 1)
-    for end in (NEAR, Z - NEAR):
-        pl.semaphore_signal(far_sem, inc=1, device_id=ring(end), device_id_type=MESH)
-    lax.fori_loop(Z // 2 - 1, Z - 1, send_out, 0)
+    def tell(step, distance):
+        for end in (distance, Z - distance):
+            pl.semaphore_signal(far_sem.at[step], inc=1, device_id=ring(end), device_id_type=MESH)
+
+    pl.semaphore_wait(barrier, 2 * NEAR + XN - 1 + YN * CORES - 1)
+    tell(0, NEAR)
+    lax.fori_loop(Z * 3 // 4 - 1, Z - 1, send_out, 0)
     pltpu.make_async_copy(out_blocks.at[Z - 1], arrived.at[Z - 1], d_recv.at[GROUPS - 1]).start()
     unfold[...] = chunk_major(GS, CH, CAP)
-    pl.semaphore_wait(far_sem, 2)
-    lax.fori_loop(0, Z // 2 - 1, send_out, 0)
+    pl.semaphore_wait(far_sem.at[0], 2)
+    tell(1, 2 * NEAR)
+    lax.fori_loop(Z // 2 - 1, Z * 3 // 4 - 1, send_out, 0)
+    pl.semaphore_wait(far_sem.at[1], 2)
+    lax.fori_loop(0, GS, send_out, 0)
 
     load_router.wait()
     load_clen.wait()
@@ -159,8 +215,13 @@
     onehot = iota((tokens, Z), 1) == ids_col
     gate_ref[...] = jax.nn.sigmoid(jnp.sum(jnp.where(onehot, logits, 0.0), axis=1, keepdims=True))
     token_total[...] = jnp.zeros_like(token_total)
-    unfold_z[...] = chunk_major(Z, CH, 2)
-    unfold_p[...] = chunk_major(PLANE, CH, 2)
+    unfold_z[...] = chunk_major(NI, CH, 2)
+    unfold_p[...] = chunk_major(NT, CH, 2)
+    image_at, caption_at = iota((2 * NI, 2 * NT), 0) // 2 % NA, iota((2 * NI, 2 * NT), 1) // 2 % NB
+    kept = jnp.ones((2 * NI, 2 * NT), f32)
+    for i, j in repeated:
+        kept = jnp.where((image_at == i) & (caption_at == j), 0.0, kept)
+    once[...] = kept
     load_in.wait()
     load_out.wait()
 
@@ -211,11 +272,23 @@
 
     def work(i, c):
         g = place(i)
+
+        @pl.when(i == GROUPS // 2)
+        def _():
+            group0 = out_blocks.at[pl.ds(0, GS)]
+            pltpu.make_async_copy(group0, group0, d_send.at[0]).wait()
+            lax.fori_loop(GS, Z // 2 - 1, send_out, 0)
+
         pltpu.make_async_copy(group(arrived, g), group(arrived, g), d_recv.at[g]).wait()
         forward(g).start()
         unpack(arrived, g, 0)
 
-        @pl.when(i > 0)
+        @pl.when(i == GROUPS // 2)
+        def _():
+            finish(place(i - 1))
+            send_group(place(i - 1))
+
+        @pl.when((i > 0) & (i != GROUPS // 2))
         def _():
             finish(place(i - 1))
 
@@ -242,11 +315,8 @@
     lax.fori_loop(0, GROUPS, work, 0)
     finish(GROUPS // 2 - 1)
 
-    def send_rest(g, c):
-        send_group(g)
-        return c
-
-    lax.fori_loop(GROUPS // 2 - 1, GROUPS, send_rest, 0)
+    send_group(GROUPS // 2 - 1)
+    send_group(GROUPS - 1)
 
     def collect(g, c):
         pltpu.make_async_copy(group(ret_arrived, g), group(ret_arrived, g), r_recv.at[g]).wait()
@@ -290,79 +360,105 @@
     units[0] = packed[0:UR]
     units[1] = packed[UR:2 * UR]
 
-    def send_images(q, c):
-        pltpu.make_async_remote_copy(
-            src_ref=units.at[0], dst_ref=image_blocks.at[q], send_sem=g_send.at[0],
-            recv_sem=g_recv.at[0], device_id=ring(offset(q)), device_id_type=MESH,
-        ).start()
-        return c
-
-    def send_texts(m, c):
-        pltpu.make_async_remote_copy(
-            src_ref=units.at[1], dst_ref=text_blocks.at[m], send_sem=g_send.at[1],
-            recv_sem=g_recv.at[1], device_id=in_plane(m), device_id_type=MESH,
-        ).start()
-        return c
-
-    lax.fori_loop(0, Z - 1, send_images, 0)
-    lax.fori_loop(1, PLANE, send_texts, 0)
-    image_blocks[Z - 1] = packed[0:UR]
-    text_blocks[0] = packed[UR:2 * UR]
+    def send_images(i, c):
+        pltpu.make_async_remote_copy(
+            src_ref=units.at[0], dst_ref=image_blocks.at[0, i], send_sem=g_send.at[0],
+            recv_sem=g_recv.at[0], device_id=along_x(0, -image_offset(Z, i)), device_id_type=MESH,
+        ).start()
+        return c
+
+    def send_texts(j, c):
+        pltpu.make_async_remote_copy(
+            src_ref=units.at[1], dst_ref=text_blocks.at[0, j], send_sem=g_send.at[1],
+            recv_sem=g_recv.at[1], device_id=along_x(0, -caption_offset(Z, j)), device_id_type=MESH,
+        ).start()
+        return c
+
+    own = 1 if NA == Z else 0
+    lax.fori_loop(1, NB, send_texts, 0)
+    lax.fori_loop(own, NA, send_images, 0)
+    if own:
+        image_blocks[0, 0] = packed[0:UR]
+    text_blocks[0, 0] = packed[UR:2 * UR]
     row_vec[...] = jnp.zeros_like(row_vec)
     col_vec[...] = jnp.zeros_like(col_vec)
 
-    def others(ref, first, sem):
-        part = ref.at[pl.ds(first, ref.shape[0] - 1)]
+    def pass_images(m, c):
+        pltpu.make_async_remote_copy(
+            src_ref=image_blocks.at[0], dst_ref=image_blocks.at[m], send_sem=h_send.at[0],
+            recv_sem=h_recv.at[0], device_id=along_x(m), device_id_type=MESH,
+        ).start()
+        return c
+
+    def pass_texts(m, c):
+        pltpu.make_async_remote_copy(
+            src_ref=text_blocks.at[0], dst_ref=text_blocks.at[m], send_sem=h_send.at[1],
+            recv_sem=h_recv.at[1], device_id=along_y(m), device_id_type=MESH,
+        ).start()
+        return c
+
+    def all_of(part, sem):
         return pltpu.make_async_copy(part, part, sem)
+
+    near_texts = text_blocks.at[0, pl.ds(min(1, NB - 1), max(1, NB - 1))]
+    near_images = image_blocks.at[0, pl.ds(own, NA - own)]
+    other_texts = text_blocks.at[pl.ds(1, YN * CORES - 1)]
+    other_images = image_blocks.at[pl.ds(min(1, XN - 1), max(1, XN - 1))]
+    if NB > 1:
+        all_of(near_texts, g_recv.at[1]).wait()
+    lax.fori_loop(1, YN * CORES, pass_texts, 0)
+    all_of(near_images, g_recv.at[0]).wait()
+    lax.fori_loop(1, XN, pass_images, 0)
 
     def lay_rows(blocks, matrix, rows_ref, n):
         rows = dot(matrix[...], blocks[...].reshape(n * UR, LANES)).astype(bf16)
         for j in range(CH):
             rows_ref[:, j * LANES:(j + 1) * LANES] = rows[j * 2 * n:(j + 1) * 2 * n]
 
-    others(text_blocks, 1, g_recv.at[1]).wait()
-    lay_rows(text_blocks, unfold_p, text_rows, PLANE)
-    others(image_blocks, 0, g_recv.at[0]).wait()
-    lay_rows(image_blocks, unfold_z, image_rows, Z)
-    by_image = jnp.exp(logit_scale * dot_nt(text_rows[...], image_rows[...]))
-    row_vec[:, 0:2 * Z] = jnp.sum(by_image, axis=0, keepdims=True)
-    by_text = jnp.exp(logit_scale * dot_nt(image_rows[...], text_rows[...]))
-    col_vec[:, 0:2 * PLANE] = jnp.sum(by_text, axis=0, keepdims=True)
-
-    def send_rows(q, c):
-        pltpu.make_async_remote_copy(
-            src_ref=row_vec, dst_ref=row_parts.at[q], send_sem=s_send.at[0],
-            recv_sem=s_recv.at[0], device_id=ring(offset(q)), device_id_type=MESH,
-        ).start()
-        return c
-
-    def send_cols(m, c):
-        pltpu.make_async_remote_copy(
-            src_ref=col_vec, dst_ref=col_parts.at[m], send_sem=s_send.at[1],
-            recv_sem=s_recv.at[1], device_id=in_plane(m), device_id_type=MESH,
-        ).start()
-        return c
-
-    lax.fori_loop(0, Z - 1, send_rows, 0)
-    lax.fori_loop(1, PLANE, send_cols, 0)
-    row_parts[Z - 1] = row_vec[...]
+    all_of(other_texts, h_recv.at[1]).wait()
+    lay_rows(text_blocks, unfold_p, text_rows, NT)
+    if XN > 1:
+        all_of(other_images, h_recv.at[0]).wait()
+    lay_rows(image_blocks, unfold_z, image_rows, NI)
+    weights = once[...] * jnp.exp(logit_scale * dot_nt(image_rows[...], text_rows[...]))
+    col_vec[:, 0:2 * NT] = jnp.sum(weights, axis=0, keepdims=True)
+    eye_rows = iota((2 * NI, 2 * NI), 0) == iota((2 * NI, 2 * NI), 1)
+    by_row = jnp.sum(weights, axis=1, keepdims=True)
+    row_vec[:, 0:2 * NI] = jnp.sum(jnp.where(eye_rows, by_row, 0.0), axis=0, keepdims=True)
+
+    def send_rows(n, c):
+        pltpu.make_async_remote_copy(
+            src_ref=row_vec, dst_ref=row_parts.at[n], send_sem=s_send.at[0], recv_sem=s_recv.at[0],
+            device_id=along_x(XN - n // NA, image_offset(Z, n % NA)), device_id_type=MESH,
+        ).start()
+        return c
+
+    def send_cols(n, c):
+        m = n // NB
+        back = (YN - m // CORES) * CORES + m % CORES
+        pltpu.make_async_remote_copy(
+            src_ref=col_vec, dst_ref=col_parts.at[n], send_sem=s_send.at[1], recv_sem=s_recv.at[1],
+            device_id=along_y(back, caption_offset(Z, n % NB)), device_id_type=MESH,
+        ).start()
+        return c
+
+    lax.fori_loop(1, NT, send_cols, 0)
+    lax.fori_loop(own, NI, send_rows, 0)
     col_parts[0] = col_vec[...]
-
-    q = iota((Z, 1, LANES), 0)
-    lane = iota((Z, 1, LANES), 2)
-    back = jnp.where((q == 0) | (q == Z - 1), q, jnp.where(q % 2 == 1, q + 1, q - 1))
-    m = iota((PLANE, 1, LANES), 0)
-    mlane = iota((PLANE, 1, LANES), 2)
-    mback = ((DP - m // CORES) % DP) * CORES + ((CORES - m % CORES) % CORES)
-
-    def mine(parts, lanes, at):
-        kept = jnp.where(lanes == at, parts, 0.0)
+    if own:
+        row_parts[0] = row_vec[...]
+
+    def mine(parts, n, i):
+        lane, at = iota((n, 1, LANES), 2), iota((n, 1, LANES), 0)
+        kept = jnp.where(lane == 2 * at + i, parts, 0.0)
         return jnp.sum(jnp.sum(kept, axis=0), axis=1, keepdims=True)
 
-    others(col_parts, 1, s_recv.at[1]).wait()
-    col_total = [mine(col_parts[...], mlane, 2 * mback + i) for i in range(2)]
-    others(row_parts, 0, s_recv.at[0]).wait()
-    row_total = [mine(row_parts[...], lane, 2 * back + i) for i in range(2)]
+    other_cols = col_parts.at[pl.ds(1, NT - 1)]
+    other_rows = row_parts.at[pl.ds(own, NI - own)]
+    all_of(other_cols, s_recv.at[1]).wait()
+    col_total = [mine(col_parts[...], NT, i) for i in range(2)]
+    all_of(other_rows, s_recv.at[0]).wait()
+    row_total = [mine(row_parts[...], NI, i) for i in range(2)]
     losses = [
         0.5 * (jnp.log(row_total[i]) - pick(i)) + 0.5 * (jnp.log(col_total[i]) - pick(i))
         for i in range(2)
@@ -373,7 +469,9 @@
     def sent(part, sem):
         pltpu.make_async_copy(part, part, sem).wait()
 
-    sent(out_blocks.at[pl.ds(0, Z - 1)], d_send)
+    for g in range(1, GROUPS):
+        count = GS - 1 if g == GROUPS - 1 else GS
+        sent(out_blocks.at[pl.ds(g * GS, count)], d_send.at[g])
     sent(ret_blocks.at[pl.ds(0, Z - 1)], r_send)
 
     def drain(g, c):
@@ -382,17 +480,23 @@
         return c
 
     lax.fori_loop(0, GROUPS, drain, 0)
-    sent(image_blocks.at[pl.ds(0, Z - 1)], g_send.at[0])
-    sent(text_blocks.at[pl.ds(1, PLANE - 1)], g_send.at[1])
-    sent(row_parts.at[pl.ds(0, Z - 1)], s_send.at[0])
-    sent(col_parts.at[pl.ds(1, PLANE - 1)], s_send.at[1])
+    all_of(near_images, g_send.at[0]).wait()
+    if NB > 1:
+        all_of(near_texts, g_send.at[1]).wait()
+    if XN > 1:
+        all_of(other_images, h_send.at[0]).wait()
+    all_of(other_texts, h_send.at[1]).wait()
+    all_of(other_rows, s_send.at[0]).wait()
+    all_of(other_cols, s_send.at[1]).wait()
 
 
 def per_device(tokens, expert_ids, caption_len, router, expert_in, expert_out, *, cfg):
     pairs, seq, width = tokens.shape
     count = pairs * seq
     Z, DP, CAP, CH, GS, FFC = cfg
-    PLANE = DP * CORES
+    XN, YN = plane_shape(DP)
+    NA, NB, _ = meeting(Z)
+    NI, NT = XN * NA, YN * CORES * NB
     GROUPS = Z // GS
     BLK = CAP * CH
     ROWS = GS * CAP
@@ -422,8 +526,8 @@
             pltpu.VMEM((hidden, width), bf16),
             pltpu.VMEM((GS * BLK, GS * BLK), bf16),
             pltpu.VMEM((GS * BLK, GS * BLK), bf16),
-            pltpu.VMEM((Z * 16, Z * 16), bf16),
-            pltpu.VMEM((PLANE * 16, PLANE * 16), bf16),
+            pltpu.VMEM((NI * 16, NI * 16), bf16),
+            pltpu.VMEM((NT * 16, NT * 16), bf16),
             pltpu.VMEM((count, 1), jnp.int32),
             pltpu.VMEM((count, 1), f32),
             blocks, blocks, blocks,
@@ -432,17 +536,18 @@
             parts, parts, parts, blocks, blocks,
             pltpu.VMEM((count, width), f32),
             pltpu.VMEM((2, 16, LANES), bf16),
-            pltpu.VMEM((Z, 16, LANES), bf16),
-            pltpu.VMEM((PLANE, 16, LANES), bf16),
-            pltpu.VMEM((2 * Z, width), bf16),
-            pltpu.VMEM((2 * PLANE, width), bf16),
+            pltpu.VMEM((XN, NA, 16, LANES), bf16),
+            pltpu.VMEM((YN * CORES, NB, 16, LANES), bf16),
+            pltpu.VMEM((2 * NI, width), bf16),
+            pltpu.VMEM((2 * NT, width), bf16),
+            pltpu.VMEM((2 * NI, 2 * NT), f32),
             pltpu.VMEM((1, LANES), f32),
             pltpu.VMEM((1, LANES), f32),
-            pltpu.VMEM((Z, 1, LANES), f32),
-            pltpu.VMEM((PLANE, 1, LANES), f32),
-            dma((6,)), pltpu.SemaphoreType.REGULAR, dma, dma((GROUPS,)), dma((GROUPS,)), dma((GROUPS,)),
+            pltpu.VMEM((NI, 1, LANES), f32),
+            pltpu.VMEM((NT, 1, LANES), f32),
+            dma((6,)), pltpu.SemaphoreType.REGULAR((2,)), dma((GROUPS,)), dma((GROUPS,)), dma((GROUPS,)), dma((GROUPS,)),
             dma((GROUPS,)), dma((GROUPS,)), dma, dma((GROUPS,)),
-            dma((2,)), dma((2,)), dma((2,)), dma((2,)),
+            dma((2,)), dma((2,)), dma((2,)), dma((2,)), dma((2,)), dma((2,)),
         ],
         compiler_params=pltpu.CompilerParams(
             collective_id=0, has_side_effects=True, vmem_limit_bytes=64 << 20

time: 135 us -> 126 us (0.933)
  Pallas kernels: 131 us -> 121 us
    pallas_call x1, Pallas kernels: 131 us -> 121 us  [per_device(): pl.pallas_call(functools.partial(kernel, cfg), out_shape=(jax.ShapeDtypeS...]
where the time goes in v3:
time: 126 us; the launch traced here: 124 us
  Pallas kernels  121 us (96%)
  local copies, waits for them, and re-layouts  2.8 us (2%)
    pallas_call x1, Pallas kernels, per_device(): pl.pallas_call(functools.partial(kernel, cfg), out_shape=(jax.ShapeDtypeS...  121 us

profile of v3, /device:TPU:6, one launch (start us, length us, event | category | flops | bytes accessed | tf_op | source)
XLA Modules:
  0.0 124.1 jit_solution(11969224965012032556)
XLA Ops:
  0.6 120.7 %expert_contrast.1 = (bf16[128,1024]{1,0:T(8,128)(2,1)}, f32[1,128]{1,0:T(1,128)}) custom-call(bf16[128,1024]{1,0:T(8,128)(2,1)} %bitcast.9, s32[2,1,64]{2,1,0:T(1,128)} %bitcast.11, s32[2]{0:T(128)} %clen_hbm.1, bf16[32,1024]{1,0:T(8,128)(2,1)} %bitcast.10, bf16[1,1024,2048]{2,1,0:T(8,128)(2,1)} %win_hbm.1, bf16[1,2048,1024]{2,1,0:T(8,128)(2,1)} %wout_hbm.1), custom_call_target="tpu_custom_call" | custom-call | flops 3221225472 | bytes 8388608 | tf_op jit(solution)/shard_map/expert_contrast/pallas_call | solution.py:509
  121.3 1.1 slice_bitcast_fusion
  122.4 1.7 %copy.10 = bf16[2,64,1024]{2,1,0:T(8,128)(2,1)} copy(bf16[2,64,1024]{2,1,0:T(8,128)(2,1)} %bitcast.8) | data formatting | bytes 524288

commit v4 on v3

--- a/solution.py
+++ b/solution.py
@@ -81,13 +81,13 @@
 
 
 def kernel(
-    cfg, tok_hbm, ids_hbm, clen_hbm, router_hbm, win_hbm, wout_hbm, out_hbm, loss_ref,
-    tok, ids, clen, router_t, out_ref, win, wout, unfold, fold, unfold_z, unfold_p, slot_col_ref, gate_ref,
+    cfg, tok_hbm, ids_hbm, clen_hbm, router_hbm, win_hbm, wout_hbm, out_hbm, loss_hbm,
+    tok, ids, clen, router_t, out_ref, loss_ref, win, wout, unfold, fold, unfold_z, unfold_p, slot_col_ref, gate_ref,
     out_blocks, arrived, sib_arrived, x_rows, total,
     own_part, send_part, sib_part, ret_blocks, ret_arrived, token_total,
     units, image_blocks, text_blocks, image_rows, text_rows, once,
     row_vec, col_vec, row_parts, col_parts,
-    w_sem, far_sem, d_send, d_recv, f_send, f_recv, p_send, p_recv, r_send, r_recv,
+    w_sem, far_sem, core_sem, d_send, d_recv, f_send, f_recv, p_send, p_recv, r_send, r_recv,
     g_send, g_recv, h_send, h_recv, s_send, s_recv,
 ):
     Z, DP, CAP, CH, GS, FFC = cfg
@@ -137,7 +137,15 @@
         return c
 
     def greet_y(m, c):
-        pl.semaphore_signal(barrier, inc=1, device_id=along_y(m), device_id_type=MESH)
+        pl.semaphore_signal(barrier, inc=1, device_id=along_y(m * CORES), device_id_type=MESH)
+        return c
+
+    def greet_other_core(m, c):
+        pl.semaphore_signal(barrier, inc=1, device_id=along_y(m * CORES + 1), device_id_type=MESH)
+        return c
+
+    def answer_other_core(m, c):
+        pl.semaphore_signal(core_sem, inc=1, device_id=along_y(m * CORES + 1), device_id_type=MESH)
         return c
 
     NEAR = Z // 8
@@ -152,7 +160,8 @@
     lax.fori_loop(1, NEAR + 1, greet_ring, 0)
     lax.fori_loop(Z - NEAR, Z, greet_ring, 0)
     lax.fori_loop(1, XN, greet_x, 0)
-    lax.fori_loop(1, YN * CORES, greet_y, 0)
+    lax.fori_loop(1, YN, greet_y, 0)
+    lax.fori_loop(0, YN * (1 - core), greet_other_core, 0)
     load_router.start()
     load_clen.start()
     load_in.start()
@@ -198,8 +207,9 @@
         for end in (distance, Z - distance):
             pl.semaphore_signal(far_sem.at[step], inc=1, device_id=ring(end), device_id_type=MESH)
 
-    pl.semaphore_wait(barrier, 2 * NEAR + XN - 1 + YN * CORES - 1)
+    pl.semaphore_wait(barrier, 2 * NEAR + XN - 1 + YN - 1 + YN * core)
     tell(0, NEAR)
+    lax.fori_loop(0, YN * core, answer_other_core, 0)
     lax.fori_loop(Z * 3 // 4 - 1, Z - 1, send_out, 0)
     pltpu.make_async_copy(out_blocks.at[Z - 1], arrived.at[Z - 1], d_recv.at[GROUPS - 1]).start()
     unfold[...] = chunk_major(GS, CH, CAP)
@@ -288,13 +298,9 @@
             finish(place(i - 1))
             send_group(place(i - 1))
 
-        @pl.when((i > 0) & (i != GROUPS // 2))
+        @pl.when((i > 0) & (i < GROUPS // 2))
         def _():
             finish(place(i - 1))
-
-        @pl.when(i > GROUPS // 2)
-        def _():
-            send_group(place(i - 1))
 
         forward(g).wait_recv()
         unpack(sib_arrived, g, ROWS)
@@ -310,12 +316,19 @@
         own_part[g] = total[0:ROWS].astype(bf16)
         send_part[g] = total[ROWS:2 * ROWS].astype(bf16)
         swap(g).start()
-        return c
+
+        @pl.when(i >= GROUPS // 2)
+        def _():
+            finish(g)
+            send_group(g)
+
+        return c
+
+    @pl.when(core == 0)
+    def _():
+        pl.semaphore_wait(core_sem, YN)
 
     lax.fori_loop(0, GROUPS, work, 0)
-    finish(GROUPS // 2 - 1)
-
-    send_group(GROUPS // 2 - 1)
     send_group(GROUPS - 1)
 
     def collect(g, c):
@@ -463,9 +476,13 @@
         0.5 * (jnp.log(row_total[i]) - pick(i)) + 0.5 * (jnp.log(col_total[i]) - pick(i))
         for i in range(2)
     ]
-    loss_ref[...] = jnp.where(iota((1, LANES), 1) == 0, losses[0], losses[1])
+    for i in range(2):
+        loss_ref[i] = jnp.sum(losses[i])
+    store_loss = pltpu.make_async_copy(loss_ref, loss_hbm, w_sem.at[1])
+    store_loss.start()
 
     store.wait()
+    store_loss.wait()
     def sent(part, sem):
         pltpu.make_async_copy(part, part, sem).wait()
 
@@ -488,6 +505,11 @@
     all_of(other_texts, h_send.at[1]).wait()
     all_of(other_rows, s_send.at[0]).wait()
     all_of(other_cols, s_send.at[1]).wait()
+
+
+def hand_over(out, loss, out_result, loss_result):
+    out_result[...] = out[...]
+    loss_result[...] = loss[...]
 
 
 def per_device(tokens, expert_ids, caption_len, router, expert_in, expert_out, *, cfg):
@@ -501,7 +523,6 @@
     BLK = CAP * CH
     ROWS = GS * CAP
     hidden = expert_in.shape[2]
-    vmem = pl.BlockSpec(memory_space=pltpu.VMEM)
     hbm = pl.BlockSpec(memory_space=pltpu.HBM)
     dma = pltpu.SemaphoreType.DMA
     blocks = pltpu.VMEM((Z, BLK, LANES), bf16)
@@ -510,18 +531,19 @@
         functools.partial(kernel, cfg),
         out_shape=(
             jax.ShapeDtypeStruct((count, width), bf16),
-            jax.ShapeDtypeStruct((1, LANES), f32),
+            jax.ShapeDtypeStruct((pairs,), f32),
         ),
         in_specs=[
             hbm, hbm, hbm, hbm, hbm, hbm,
         ],
-        out_specs=(hbm, vmem),
+        out_specs=(hbm, hbm),
         scratch_shapes=[
             pltpu.VMEM((count, width), bf16),
             pltpu.VMEM((pairs, 1, seq), jnp.int32),
             pltpu.SMEM((pairs,), jnp.int32),
             pltpu.VMEM((Z, width), bf16),
             pltpu.VMEM((count, width), bf16),
+            pltpu.SMEM((pairs,), f32),
             pltpu.VMEM((width, hidden), bf16),
             pltpu.VMEM((hidden, width), bf16),
             pltpu.VMEM((GS * BLK, GS * BLK), bf16),
@@ -545,7 +567,7 @@
             pltpu.VMEM((1, LANES), f32),
             pltpu.VMEM((NI, 1, LANES), f32),
             pltpu.VMEM((NT, 1, LANES), f32),
-            dma((6,)), pltpu.SemaphoreType.REGULAR((2,)), dma((GROUPS,)), dma((GROUPS,)), dma((GROUPS,)), dma((GROUPS,)),
+            dma((6,)), pltpu.SemaphoreType.REGULAR((2,)), pltpu.SemaphoreType.REGULAR, dma((GROUPS,)), dma((GROUPS,)), dma((GROUPS,)), dma((GROUPS,)),
             dma((GROUPS,)), dma((GROUPS,)), dma, dma((GROUPS,)),
             dma((2,)), dma((2,)), dma((2,)), dma((2,)), dma((2,)), dma((2,)),
         ],
@@ -564,7 +586,19 @@
         expert_in,
         expert_out,
     )
-    return out.reshape(pairs, seq, width), loss[0, :pairs]
+    vmem = pl.BlockSpec(memory_space=pltpu.VMEM)
+    out, loss = pl.pallas_call(
+        hand_over,
+        out_shape=(
+            jax.ShapeDtypeStruct((count, width), bf16),
+            jax.ShapeDtypeStruct((pairs,), f32),
+        ),
+        in_specs=[vmem, vmem],
+        out_specs=(vmem, vmem),
+        compiler_params=pltpu.CompilerParams(vmem_limit_bytes=64 << 20),
+        name="hand_over",
+    )(out, loss)
+    return out.reshape(pairs, seq, width), loss
 
 
 def solution(mesh, cap=6, group=8, ff_chunk=512):

time: 126 us -> 125 us (level)
  local copies, waits for them, and re-layouts: 2.8 us -> 0 us
    pallas_call x0 -> x1, Pallas kernels: none -> 1.68 us  [per_device(): pl.pallas_call(hand_over, out_shape=(jax.ShapeDtypeStruct((count, width),...]
    unnamed x1 -> x0, local copies, waits for them, and re-layouts: 1.67 us -> none
where the time goes in v4:
time: 125 us; the launch traced here: 123 us
  Pallas kernels  122 us (98%)
    pallas_call x1, Pallas kernels, per_device(): pl.pallas_call(functools.partial(kernel, cfg), out_shape=(jax.ShapeDtypeS...  120 us

profile of v4, /device:TPU:6, one launch (start us, length us, event | category | flops | bytes accessed | tf_op | source)
XLA Modules:
  0.0 122.5 jit_solution(3242881772977449807)
XLA Ops:
  0.6 120.2 %expert_contrast.1 = (bf16[128,1024]{1,0:T(8,128)(2,1)}, f32[2]{0:T(128)}) custom-call(bf16[128,1024]{1,0:T(8,128)(2,1)} %bitcast.6, s32[2,1,64]{2,1,0:T(1,128)} %bitcast.9, s32[2]{0:T(128)} %clen_hbm.1, bf16[32,1024]{1,0:T(8,128)(2,1)} %bitcast.8, bf16[1,1024,2048]{2,1,0:T(8,128)(2,1)} %win_hbm.1, bf16[1,2048,1024]{2,1,0:T(8,128)(2,1)} %wout_hbm.1), custom_call_target="tpu_custom_call" | custom-call | flops 3221225472 | bytes 8388608 | tf_op jit(solution)/shard_map/expert_contrast/pallas_call | solution.py:530
  120.8 1.7 %hand_over.1 = (bf16[128,1024]{1,0:T(8,128)(2,1)}, f32[2]{0:T(128)}) custom-call(bf16[128,1024]{1,0:T(8,128)(2,1)} %get-tuple-element.6.out, f32[2]{0:T(128)} %get-tuple-element.7.loss), custom_call_target="tpu_custom_call" | custom-call | tf_op jit(solution)/shard_map/hand_over/pallas_call | solution.py:590

commit v5 on v4

--- a/solution.py
+++ b/solution.py
@@ -124,7 +124,8 @@
     sibling = {"dp": dp, "expert": z * CORES + (1 - core)}
 
     def offset(q):
-        return jnp.where(q % 2 == 1, Z // 2 - (q + 1) // 2, lax.rem(q // 2 + Z // 2, Z))
+        up = jnp.where(q % 2 == 1, Z // 2 - (q + 1) // 2, lax.rem(q // 2 + Z // 2, Z))
+        return lax.rem(Z + up * (1 - 2 * core), Z)
 
     barrier = pltpu.get_barrier_semaphore()
 
@@ -175,7 +176,7 @@
     upto = (iota((tokens, tokens), 0) <= iota((tokens, tokens), 1)).astype(bf16)
     running = dot(onehot_t.astype(bf16), upto)
     position = jnp.sum(jnp.where(onehot_t, running, 0.0), axis=0, keepdims=True).astype(jnp.int32) - 1
-    ahead = ids_row - z
+    ahead = (ids_row - z) * (1 - 2 * core)
     ahead = jnp.where(ahead < 0, ahead + Z, ahead)
     signed = jnp.where(ahead > Z // 2, ahead - Z, ahead)
     away = jnp.abs(signed)
@@ -194,7 +195,7 @@
         out_blocks[pl.ds(g * GS, GS)] = dot(fold[...], stacked).astype(bf16).reshape(GS, BLK, LANES)
         return c
 
-    lax.fori_loop(0, GROUPS, pack, 0)
+    lax.fori_loop(0, GROUPS // 2, pack, 0)
 
     def send_out(q, c):
         pltpu.make_async_remote_copy(
@@ -212,10 +213,11 @@
     lax.fori_loop(0, YN * core, answer_other_core, 0)
     lax.fori_loop(Z * 3 // 4 - 1, Z - 1, send_out, 0)
     pltpu.make_async_copy(out_blocks.at[Z - 1], arrived.at[Z - 1], d_recv.at[GROUPS - 1]).start()
-    unfold[...] = chunk_major(GS, CH, CAP)
+    lax.fori_loop(GROUPS // 2, GROUPS, pack, 0)
     pl.semaphore_wait(far_sem.at[0], 2)
     tell(1, 2 * NEAR)
     lax.fori_loop(Z // 2 - 1, Z * 3 // 4 - 1, send_out, 0)
+    unfold[...] = chunk_major(GS, CH, CAP)
     pl.semaphore_wait(far_sem.at[1], 2)
     lax.fori_loop(0, GS, send_out, 0)
 
@@ -403,7 +405,8 @@
         ).start()
         return c
 
-    def pass_texts(m, c):
+    def pass_texts(i, c):
+        m = lax.rem(i + YN, YN * CORES)
         pltpu.make_async_remote_copy(
             src_ref=text_blocks.at[0], dst_ref=text_blocks.at[m], send_sem=h_send.at[1],
             recv_sem=h_recv.at[1], device_id=along_y(m), device_id_type=MESH,
@@ -419,7 +422,8 @@
     other_images = image_blocks.at[pl.ds(min(1, XN - 1), max(1, XN - 1))]
     if NB > 1:
         all_of(near_texts, g_recv.at[1]).wait()
-    lax.fori_loop(1, YN * CORES, pass_texts, 0)
+    lax.fori_loop(0, YN, pass_texts, 0)
+    lax.fori_loop(YN + 1, YN * CORES, pass_texts, 0)
     all_of(near_images, g_recv.at[0]).wait()
     lax.fori_loop(1, XN, pass_images, 0)
 
@@ -439,24 +443,29 @@
     by_row = jnp.sum(weights, axis=1, keepdims=True)
     row_vec[:, 0:2 * NI] = jnp.sum(jnp.where(eye_rows, by_row, 0.0), axis=0, keepdims=True)
 
-    def send_rows(n, c):
+    def send_rows(i, c):
+        block, m = i // XN, lax.rem(i + XN // 2, XN)
         pltpu.make_async_remote_copy(
-            src_ref=row_vec, dst_ref=row_parts.at[n], send_sem=s_send.at[0], recv_sem=s_recv.at[0],
-            device_id=along_x(XN - n // NA, image_offset(Z, n % NA)), device_id_type=MESH,
+            src_ref=row_vec, dst_ref=row_parts.at[m * NA + block], send_sem=s_send.at[0], recv_sem=s_recv.at[0],
+            device_id=along_x(XN - m, image_offset(Z, block)), device_id_type=MESH,
         ).start()
         return c
 
-    def send_cols(n, c):
-        m = n // NB
+    def send_cols(i, c):
+        block, m = lax.rem(i // (YN * CORES) + 1, NB), lax.rem(i + YN, YN * CORES)
         back = (YN - m // CORES) * CORES + m % CORES
         pltpu.make_async_remote_copy(
-            src_ref=col_vec, dst_ref=col_parts.at[n], send_sem=s_send.at[1], recv_sem=s_recv.at[1],
-            device_id=along_y(back, caption_offset(Z, n % NB)), device_id_type=MESH,
+            src_ref=col_vec, dst_ref=col_parts.at[m * NB + block], send_sem=s_send.at[1], recv_sem=s_recv.at[1],
+            device_id=along_y(back, caption_offset(Z, block)), device_id_type=MESH,
         ).start()
         return c
 
-    lax.fori_loop(1, NT, send_cols, 0)
-    lax.fori_loop(own, NI, send_rows, 0)
+    own_col = (NB - 1) * YN * CORES + YN
+    lax.fori_loop(0, own_col, send_cols, 0)
+    lax.fori_loop(own_col + 1, NT, send_cols, 0)
+    own_row = (XN - XN // 2) % XN if own else NI
+    lax.fori_loop(0, own_row, send_rows, 0)
+    lax.fori_loop(own_row + 1, NI, send_rows, 0)
     col_parts[0] = col_vec[...]
     if own:
         row_parts[0] = row_vec[...]

time: 125 us -> 124 us (level)
  no operation moved by 1% of the time
where the time goes in v5:
time: 124 us; the launch traced here: 122 us
  Pallas kernels  121 us (98%)
    pallas_call x1, Pallas kernels, per_device(): pl.pallas_call(functools.partial(kernel, cfg), out_shape=(jax.ShapeDtypeS...  120 us

profile of v5, /device:TPU:6, one launch (start us, length us, event | category | flops | bytes accessed | tf_op | source)
XLA Modules:
  0.0 122.0 jit_solution(4923200967103066779)
XLA Ops:
  0.6 119.7 %expert_contrast.1 = (bf16[128,1024]{1,0:T(8,128)(2,1)}, f32[2]{0:T(128)}) custom-call(bf16[128,1024]{1,0:T(8,128)(2,1)} %bitcast.6, s32[2,1,64]{2,1,0:T(1,128)} %bitcast.9, s32[2]{0:T(128)} %clen_hbm.1, bf16[32,1024]{1,0:T(8,128)(2,1)} %bitcast.8, bf16[1,1024,2048]{2,1,0:T(8,128)(2,1)} %win_hbm.1, bf16[1,2048,1024]{2,1,0:T(8,128)(2,1)} %wout_hbm.1), custom_call_target="tpu_custom_call" | custom-call | flops 3221225472 | bytes 8388608 | tf_op jit(solution)/shard_map/expert_contrast/pallas_call | solution.py:539
  120.4 1.7 %hand_over.1 = (bf16[128,1024]{1,0:T(8,128)(2,1)}, f32[2]{0:T(128)}) custom-call(bf16[128,1024]{1,0:T(8,128)(2,1)} %get-tuple-element.6.out, f32[2]{0:T(128)} %get-tuple-element.7.loss), custom_call_target="tpu_custom_call" | custom-call | tf_op jit(solution)/shard_map/hand_over/pallas_call | solution.py:599
